TPU v7x, 256 devices: a whole 4x4x8 slice. The times are simulated.
256 devices in a mesh: rows: 32 (over y, x, core), cols: 8 (over z).
Axes of the slice: x: 4, y: 4, z: 8, core: 2. Of those that a mesh axis runs over, the one named last changes fastest.
Arguments:
- latent: float32 [2048, 16384], P('rows', 'cols'), may hold values from -3 to 3
- counts: int32 [2048, 16384], P('rows', 'cols'), may hold values from 0 to 39
- exposure: int32 [2048, 16384], P('rows', 'cols'), may hold values from 1 to 32
Outputs:
- newton_step: float32 [2048, 16384], P('rows', 'cols')
- residual: float32 [2048, 16384], P('rows', 'cols')
- direction: float32 [2048, 16384], P('rows', 'cols')
All inputs are finite; a program needn't handle non-finite values.
Results may differ from a plain program's by a relative error of at most 0.0003.
Values sent between devices are 32-bit elements; how exact they have to be, the bound alone decides.
No kernel may reach another device: no remote copies, remote signals or barrier semaphores. Data moves between devices by JAX's collectives and lax.ppermute only.
A program may use at most 128 MiB of HBM per device.

v0:
```python
import math
import jax
import jax.numpy as jnp
from jax import lax
from jax.sharding import PartitionSpec as P

dispersion = 4.0
prior_scale = 0.25
kappa_sq = 0.05
weight_shift = 1.0
highest = lax.Precision.HIGHEST


def extended(cells, sides, width):
    for axis, dim in sides:
        count = lax.axis_size(axis)
        ends = count - 1
        head = lax.slice_in_dim(cells, 0, width, axis=dim)
        tail = lax.slice_in_dim(cells, cells.shape[dim] - width, cells.shape[dim], axis=dim)
        cells = jnp.concatenate(
            [
                lax.ppermute(tail, axis, [(i, (i + 1) % count) for i in range(ends)]),
                cells,
                lax.ppermute(head, axis, [((i + 1) % count, i) for i in range(ends)]),
            ],
            axis=dim,
        )
    return cells


def dft_table(length):
    index_line = lax.iota(jnp.int32, length)
    product = index_line[:, None] * index_line[None, :] % length
    angle = 2.0 * math.pi / length * product.astype(jnp.float32)
    return (jnp.cos(angle), jnp.sin(angle))


def twiddle_table(outer_len, inner_len):
    product = lax.iota(jnp.int32, outer_len)[:, None] * lax.iota(jnp.int32, inner_len)[None, :]
    angle = 2.0 * math.pi / (outer_len * inner_len) * product.astype(jnp.float32)
    return (jnp.cos(angle), jnp.sin(angle))


def left_apply(table, data):
    return jnp.dot(table, data, precision=highest)


def middle_apply(table, data):
    return jnp.einsum("ka,lab->lkb", table, data, precision=highest)


def last_apply(data, table):
    line_rows, outer_len, inner_len = data.shape
    flat = jnp.dot(data.reshape(line_rows * outer_len, inner_len), table, precision=highest)
    return flat.reshape(line_rows, outer_len, inner_len)


def split_lengths(total_cols):
    inner_len = math.gcd(total_cols, 128)
    return (total_cols // inner_len, inner_len)


def columns_forward(real_part, imag_part):
    line_rows, total_cols = real_part.shape
    outer_len, inner_len = split_lengths(total_cols)
    outer_cos, outer_sin = dft_table(outer_len)
    inner_cos, inner_sin = dft_table(inner_len)
    twist_cos, twist_sin = twiddle_table(outer_len, inner_len)
    real_cube = real_part.reshape(line_rows, outer_len, inner_len)
    imag_cube = imag_part.reshape(line_rows, outer_len, inner_len)
    section_real = middle_apply(outer_cos, real_cube) + middle_apply(outer_sin, imag_cube)
    section_imag = middle_apply(outer_cos, imag_cube) - middle_apply(outer_sin, real_cube)
    turned_real = section_real * twist_cos + section_imag * twist_sin
    turned_imag = section_imag * twist_cos - section_real * twist_sin
    final_real = last_apply(turned_real, inner_cos) + last_apply(turned_imag, inner_sin)
    final_imag = last_apply(turned_imag, inner_cos) - last_apply(turned_real, inner_sin)
    return (final_real.reshape(line_rows, total_cols), final_imag.reshape(line_rows, total_cols))


def columns_inverse(real_part, imag_part):
    line_rows, total_cols = real_part.shape
    outer_len, inner_len = split_lengths(total_cols)
    outer_cos, outer_sin = dft_table(outer_len)
    inner_cos, inner_sin = dft_table(inner_len)
    twist_cos, twist_sin = twiddle_table(outer_len, inner_len)
    real_cube = real_part.reshape(line_rows, outer_len, inner_len)
    imag_cube = imag_part.reshape(line_rows, outer_len, inner_len)
    section_real = last_apply(real_cube, inner_cos) - last_apply(imag_cube, inner_sin)
    section_imag = last_apply(imag_cube, inner_cos) + last_apply(real_cube, inner_sin)
    turned_real = section_real * twist_cos - section_imag * twist_sin
    turned_imag = section_imag * twist_cos + section_real * twist_sin
    final_real = middle_apply(outer_cos, turned_real) - middle_apply(outer_sin, turned_imag)
    final_imag = middle_apply(outer_cos, turned_imag) + middle_apply(outer_sin, turned_real)
    return (final_real.reshape(line_rows, total_cols), final_imag.reshape(line_rows, total_cols))


def inverse_symbol(row_freq, col_freq, band_rows, total_cols):
    row_sine = jnp.sin(math.pi * row_freq.astype(jnp.float32) / band_rows)
    col_sine = jnp.sin(math.pi * col_freq.astype(jnp.float32) / total_cols)
    inner_term = kappa_sq + 4.0 * row_sine * row_sine + 4.0 * col_sine * col_sine
    symbol = prior_scale * inner_term * inner_term + weight_shift
    quarter = total_cols // 4
    retained = (col_freq < quarter) | (col_freq > total_cols - quarter)
    weight = jnp.where(retained, 1.0 / symbol, 1.0)
    return weight / float(band_rows * total_cols)


def frequency_of(position, outer_len, inner_len):
    return position // inner_len + outer_len * (position % inner_len)


def precondition(grid_field):
    band_rows, block_cols = grid_field.shape
    col_parts = lax.axis_size("cols")
    col_index = lax.axis_index("cols")
    total_cols = block_cols * col_parts
    outer_len, inner_len = split_lengths(total_cols)
    row_cos, row_sin = dft_table(band_rows)
    spectrum = jnp.stack([left_apply(row_cos, grid_field), -left_apply(row_sin, grid_field)])
    whole_lines = lax.all_to_all(spectrum, "cols", split_axis=1, concat_axis=2, tiled=True)
    line_rows = band_rows // col_parts
    spec_real, spec_imag = columns_forward(whole_lines[0], whole_lines[1])
    row_freq = col_index * line_rows + lax.iota(jnp.int32, line_rows)
    col_freq = frequency_of(lax.iota(jnp.int32, total_cols), outer_len, inner_len)
    spectral_scale = inverse_symbol(row_freq[:, None], col_freq[None, :], band_rows, total_cols)
    back_real, back_imag = columns_inverse(spec_real * spectral_scale, spec_imag * spectral_scale)
    blocks = lax.all_to_all(
        jnp.stack([back_real, back_imag]), "cols", split_axis=2, concat_axis=1, tiled=True
    )
    return left_apply(row_cos, blocks[0]) - left_apply(row_sin, blocks[1])


def prior_apply(grid_field):
    padded = extended(grid_field, (("rows", 0), ("cols", 1)), 2)
    row_count, col_count = grid_field.shape

    def offset_view(shift_row, shift_col):
        return padded[
            2 + shift_row : 2 + shift_row + row_count, 2 + shift_col : 2 + shift_col + col_count
        ]

    centre = kappa_sq + 4.0
    nearest = offset_view(1, 0) + offset_view(-1, 0) + offset_view(0, 1) + offset_view(0, -1)
    diagonal = offset_view(1, 1) + offset_view(1, -1) + offset_view(-1, 1) + offset_view(-1, -1)
    distant = offset_view(2, 0) + offset_view(-2, 0) + offset_view(0, 2) + offset_view(0, -2)
    return prior_scale * (
        (centre * centre + 4.0) * grid_field - 2.0 * centre * nearest + 2.0 * diagonal + distant
    )


def on_device(latent, counts, exposure):
    mean_rate = exposure.astype(jnp.float32) * jnp.exp(latent)
    fisher = dispersion * mean_rate / (dispersion + mean_rate)
    score = (counts.astype(jnp.float32) - mean_rate) * dispersion / (dispersion + mean_rate)
    gradient = score - prior_apply(latent)
    first_search = precondition(gradient)
    first_product = lax.psum(jnp.sum(gradient * first_search), ("rows", "cols"))
    image = prior_apply(first_search) + fisher * first_search
    curvature = lax.psum(jnp.sum(first_search * image), ("rows", "cols"))
    step_size = first_product / curvature
    residual = gradient - step_size * image
    next_search = precondition(residual)
    next_product = lax.psum(jnp.sum(residual * next_search), ("rows", "cols"))
    newton_step = step_size * first_search
    direction = next_search + next_product / first_product * first_search
    return (newton_step, residual, direction)


def solution(mesh):
    placed = (P("rows", "cols"), P("rows", "cols"), P("rows", "cols"))
    return jax.shard_map(
        on_device,
        mesh=mesh,
        in_specs=placed,
        out_specs=(P("rows", "cols"), P("rows", "cols"), P("rows", "cols")),
        check_vma=False,
    )
```

profile of v0, /device:TPU:1, one launch (start us, length us, event | category | flops | bytes accessed | tf_op | source)
XLA Modules:
  0.0 564.2 jit_solution(15677637600210697787)
XLA Ops:
  0.6 0.9 fusion.333
  1.5 5.1 collective-permute-start
  6.7 1.9 collective-permute-start.1
  8.6 1.1 constant_dynamic-update-slice_fusion.1
  10.6 1.3 collective-permute-start.2
  11.9 4.0 collective-permute-start.3
  15.9 1.0 collective-permute-done.3
  17.0 1.5 pad_maximum_fusion.4
  18.4 2.9 fusion.34
  22.8 1.8 copy.128
  24.6 9.9 %all-to-all-start = ((f32[2,64,2048]{2,0,1:T(2,128)}), f32[2,64,2048]{2,0,1:T(2,128)S(1)}, u32[]{:S(2)}, u32[]{:S(2)}) async-start(f32[2,64,2048]{2,0,1:T(2,128)} %copy.128), calls=%async_computation | async-start | bytes 2097152 | tf_op jit(solution)/shard_map/all_to_all | solution.py:120
  35.6 27.9 %all-to-all-done = f32[2,64,2048]{2,0,1:T(2,128)S(1)} async-done(((f32[2,64,2048]{2,0,1:T(2,128)}), f32[2,64,2048]{2,0,1:T(2,128)S(1)}, u32[]{:S(2)}, u32[]{:S(2)}) %all-to-all-start) | async-done | bytes 1048608 | tf_op jit(solution)/shard_map/all_to_all | solution.py:120
  64.3 1.1 fusion.102
  65.4 1.1 fusion.104
  66.6 1.1 fusion.12
  67.7 1.1 fusion.13
  68.8 1.2 fusion.54
  70.0 1.2 fusion.53
  71.2 1.3 fusion.10
  72.5 0.9 fusion.96
  73.4 1.8 fusion.11
  76.9 0.9 convolution_subtract_fusion.7
  80.5 0.9 stack_reshape.13
  82.6 1.1 pad_maximum_fusion.1
  83.7 14.7 %copy.146 = f32[2,8,16384]{1,0,2:T(2,128)} copy(f32[2,8,16384]{2,1,0:T(8,128)S(1)} %pad_maximum_fusion.1) | data formatting | bytes 2097152 | tf_op jit(solution)/shard_map/stack | solution.py:128
  98.4 28.3 %reshape.237 = f32[8,1,32768]{2,1,0:T(1,128)S(1)} reshape(f32[16384,2,8]{2,1,0:T(2,128)} %bitcast.148) | data formatting | bytes 2097152
  126.7 31.4 %all_to_all.60 = f32[8,1,32768]{2,1,0:T(1,128)S(1)} all-to-all(f32[8,1,32768]{2,1,0:T(1,128)S(1)} %reshape.237), channel_id=1, replica_groups=mesh['rows'=32,'cols'=8] {'cols'}, dimensions={0} | all-to-all | bytes 2097152 | tf_op jit(solution)/shard_map/all_to_all | solution.py:127
  158.7 3.2 reduce
  161.9 32.3 %reshape.238 = f32[16384,2,8]{2,1,0:T(2,128)} reshape(f32[8,32768]{1,0:T(8,128)S(1)} %reduce) | data formatting | bytes 2097152
  194.2 13.2 %copy.194 = f32[2,8,8,2048]{3,2,1,0:T(8,128)S(1)} copy(f32[2,8,8,2048]{1,0,3,2:T(2,128)} %bitcast.149) | data formatting | bytes 2097152 | tf_op jit(solution)/shard_map/all_to_all | solution.py:127
  207.5 0.9 fusion.47
  208.5 0.9 convolution_subtract_fusion.1
  209.4 1.9 collective-permute-start.5
  211.3 2.4 collective-permute-start.4
  213.8 2.6 collective-permute-done.4
  216.5 1.3 collective-permute-start.6
  217.8 4.0 collective-permute-start.7
  221.8 1.0 collective-permute-done.7
  223.1 1.8 multiply_reduce_fusion.1
  224.9 79.0 %all-reduce = (f32[]{:T(128)}, f32[]{:T(128)}) all-reduce(f32[]{:T(128)} %get-tuple-element.4, f32[]{:T(128)} %get-tuple-element.3), channel_id=1, replica_groups=mesh['rows'=32,'cols'=8] {'rows','cols'}, use_global_device_ids=true, to_apply=%region_1.2 | all-reduce | flops 2 | bytes 16 | tf_op jit(solution)/shard_map/psum | solution.py:157
  307.6 31.7 %all_to_all.61 = f32[2,64,2048]{2,0,1:T(2,128)S(1)} all-to-all(f32[2,64,2048]{2,0,1:T(2,128)S(1)} %copy.150), channel_id=1, replica_groups=mesh['rows'=32,'cols'=8] {'cols'}, dimensions={1} | all-to-all | bytes 2097152 | tf_op jit(solution)/shard_map/all_to_all | solution.py:120
  340.2 1.1 fusion.90
  341.4 1.1 fusion.92
  342.5 1.1 fusion.6
  343.6 1.1 fusion.7
  344.7 1.2 fusion.58
  345.9 1.2 fusion.57
  347.1 1.3 fusion.4
  349.3 1.3 fusion.5
  350.6 1.1 fusion.87
  352.6 0.9 convolution_subtract_fusion.3
  356.0 1.0 copy.165
  356.9 1.9 stack_reshape.15
  360.0 1.1 pad_maximum_fusion.3
  361.1 14.7 %copy.166 = f32[2,8,16384]{1,0,2:T(2,128)} copy(f32[2,8,16384]{2,1,0:T(8,128)S(1)} %pad_maximum_fusion.3) | data formatting | bytes 2097152 | tf_op jit(solution)/shard_map/stack | solution.py:128
  375.8 28.3 %reshape.239 = f32[8,1,32768]{2,1,0:T(1,128)S(1)} reshape(f32[16384,2,8]{2,1,0:T(2,128)} %bitcast.150) | data formatting | bytes 2097152
  404.1 28.8 %all_to_all.62 = f32[8,1,32768]{2,1,0:T(1,128)} all-to-all(f32[8,1,32768]{2,1,0:T(1,128)S(1)} %reshape.239), channel_id=1, replica_groups=mesh['rows'=32,'cols'=8] {'cols'}, dimensions={0} | all-to-all | bytes 2097152 | tf_op jit(solution)/shard_map/all_to_all | solution.py:127
  432.9 4.4 reduce.1
  437.3 32.1 %reshape.240 = f32[16384,2,8]{2,1,0:T(2,128)} reshape(f32[8,32768]{1,0:T(8,128)S(1)} %reduce.1) | data formatting | bytes 2097152
  469.4 13.2 %copy.195 = f32[2,8,8,2048]{3,2,1,0:T(8,128)S(1)} copy(f32[2,8,8,2048]{1,0,3,2:T(2,128)} %bitcast.151) | data formatting | bytes 2097152 | tf_op jit(solution)/shard_map/all_to_all | solution.py:127
  482.7 0.9 fusion.44
  483.6 1.6 multiply_reduce_fusion
  485.2 76.5 %psum.23 = f32[]{:T(128)} all-reduce(f32[]{:T(128)} %get-tuple-element.30), channel_id=1, replica_groups=mesh['rows'=32,'cols'=8] {'rows','cols'}, use_global_device_ids=true, to_apply=%region_5.6 | all-reduce | flops 1 | bytes 8 | tf_op jit(solution)/shard_map/psum | solution.py:163
  562.9 1.1 multiply_add_fusion
  (59 shorter events, 19.5 us)
Async XLA Ops:
  1.5 8.2 %collective-permute-start = (f32[2,2048]{1,0:T(2,128)S(1)}, f32[2,2048]{1,0:T(2,128)S(1)}, u32[]{:S(2)}, u32[]{:S(2)}) collective-permute-start(f32[2,2048]{1,0:T(2,128)S(1)} %get-tuple-element.28), channel_id=1, source_target_pairs={{8,0},{16,8},{24,16},{32,24},{40,32},{48,40},{56,48},{64,56},{72,6... | collective-permute-start | bytes 49160 | tf_op jit(solution)/shard_map/ppermute | solution.py:24
  6.7 3.1 collective-permute-start.1
  10.6 5.3 collective-permute-start.2
  11.9 5.0 collective-permute-start.3
  24.6 38.8 %all-to-all-start = ((f32[2,64,2048]{2,0,1:T(2,128)}), f32[2,64,2048]{2,0,1:T(2,128)S(1)}, u32[]{:S(2)}, u32[]{:S(2)}) async-start(f32[2,64,2048]{2,0,1:T(2,128)} %copy.128), calls=%async_computation | async-start | bytes 2097152 | tf_op jit(solution)/shard_map/all_to_all | solution.py:120
  194.2 28.9 %copy-start = (f32[64,2048]{1,0:T(8,128)S(1)}, f32[64,2048]{1,0:T(8,128)}, u32[]{:S(2)}) copy-start(f32[64,2048]{1,0:T(8,128)} %param.3) | copy-start | bytes 1572868
  194.2 28.9 %copy-start.2 = (s32[64,2048]{1,0:T(8,128)S(1)}, s32[64,2048]{1,0:T(8,128)}, u32[]{:S(2)}) copy-start(s32[64,2048]{1,0:T(8,128)} %param.5) | copy-start | bytes 1572868
  209.4 4.3 collective-permute-start.5
  211.3 5.1 collective-permute-start.4
  216.5 5.3 collective-permute-start.6
  217.8 5.0 collective-permute-start.7
  305.3 178.3 %copy-start.1 = (f32[64,2048]{1,0:T(8,128)}, f32[64,2048]{1,0:T(8,128)S(1)}, u32[]{:S(2)}) copy-start(f32[64,2048]{1,0:T(8,128)S(1)} %multiply_subtract_fusion.2) | copy-start | bytes 1572868
where the time goes:
time: 569 us; the launch traced here: 564 us
  blocking collectives  247 us (43%)
  local copies, waits for them, and re-layouts  189 us (33%)
  matrix products  40.4 us (7%)
  waiting for transfers between devices  32.6 us (6%)
  starting transfers between devices  31.8 us (6%)
  other arithmetic  19.3 us (3%)
    unnamed x11, local copies, waits for them, and re-layouts  122 us
    psum x1, blocking collectives, on_device(): first_product = lax.psum(jnp.sum(gradient * first_search), ('rows', 'cols'))  79 us
    psum x1, blocking collectives, on_device(): next_product = lax.psum(jnp.sum(residual * next_search), ('rows', 'cols'))  76.5 us
    all_to_all x2, blocking collectives, precondition(): lax.all_to_all(jnp.stack([back_real, back_imag]), 'cols', split_axis=2, c...  60.2 us
    another operation x6, local copies, waits for them, and re-layouts, precondition(): jnp.stack([back_real, back_imag])  32.4 us
    all_to_all x1, blocking collectives, precondition(): lax.all_to_all(spectrum, 'cols', split_axis=1, concat_axis=2, tiled=True)  31.7 us
    all_to_all x1, waiting for transfers between devices, precondition(): lax.all_to_all(spectrum, 'cols', split_axis=1, concat_axis=2, tiled=True)  27.9 us
    all_to_all x3, local copies, waits for them, and re-layouts, precondition(): lax.all_to_all(jnp.stack([back_real, back_imag]), 'cols', split_axis=2, c...  27 us
  transfers between devices with their start and end apart: 9, of which 5 were waited for; matrix products, arithmetic and copies ran while one was open for 0% of the time, Pallas kernels for 0%

commit v1 on v0

--- a/solution.py
+++ b/solution.py
@@ -117,7 +117,17 @@
     outer_len, inner_len = split_lengths(total_cols)
     row_cos, row_sin = dft_table(band_rows)
     spectrum = jnp.stack([left_apply(row_cos, grid_field), -left_apply(row_sin, grid_field)])
-    whole_lines = lax.all_to_all(spectrum, "cols", split_axis=1, concat_axis=2, tiled=True)
+
+    def manage_the_boxes(u, shard_axis, dim_k, on_dim):
+        frame_out = lax.all_to_all(
+            jnp.stack(jnp.split(u, lax.axis_size(shard_axis), axis=dim_k), axis=0),
+            axis_name=shard_axis,
+            split_axis=0,
+            concat_axis=0,
+        )
+        return jnp.concatenate(frame_out, axis=on_dim)
+
+    whole_lines = manage_the_boxes(spectrum, "cols", 1, 2)
     line_rows = band_rows // col_parts
     spec_real, spec_imag = columns_forward(whole_lines[0], whole_lines[1])
     row_freq = col_index * line_rows + lax.iota(jnp.int32, line_rows)

time: 569 us -> 571 us (level)
  no operation moved by 1% of the time
where the time goes in v1:
time: 571 us; the launch traced here: 567 us
  blocking collectives  248 us (43%)
  local copies, waits for them, and re-layouts  186 us (33%)
  matrix products  40.2 us (7%)
  waiting for transfers between devices  32.7 us (6%)
  starting transfers between devices  31.7 us (6%)
  other arithmetic  24.6 us (4%)
    unnamed x11, local copies, waits for them, and re-layouts  122 us
    psum x1, blocking collectives, on_device(): first_product = lax.psum(jnp.sum(gradient * first_search), ('rows', 'cols'))  79 us
    psum x1, blocking collectives, on_device(): next_product = lax.psum(jnp.sum(residual * next_search), ('rows', 'cols'))  76.6 us
    all_to_all x2, blocking collectives, precondition(): lax.all_to_all(jnp.stack([back_real, back_imag]), 'cols', split_axis=2, c...  60.2 us
    another operation x6, local copies, waits for them, and re-layouts, precondition(): jnp.stack([back_real, back_imag])  32.4 us
    all_to_all x1, blocking collectives, manage_the_boxes(): lax.all_to_all(jnp.stack(jnp.split(u, lax.axis_size(shard_axis), axis=dim...  31.8 us
    all_to_all x1, waiting for transfers between devices, manage_the_boxes(): lax.all_to_all(jnp.stack(jnp.split(u, lax.axis_size(shard_axis), axis=dim...  28 us
    all_to_all x3, local copies, waits for them, and re-layouts, precondition(): lax.all_to_all(jnp.stack([back_real, back_imag]), 'cols', split_axis=2, c...  27 us
  transfers between devices with their start and end apart: 9, of which 5 were waited for; matrix products, arithmetic and copies ran while one was open for 0% of the time, Pallas kernels for 0%

profile of v1, /device:TPU:1, one launch (start us, length us, event | category | flops | bytes accessed | tf_op | source)
XLA Modules:
  0.0 566.8 jit_solution(3623217719526018424)
XLA Ops:
  0.6 0.9 fusion.379
  1.5 5.1 collective-permute-start
  6.7 1.9 collective-permute-start.1
  8.6 1.1 constant_dynamic-update-slice_fusion.1
  10.6 1.3 collective-permute-start.2
  11.9 4.0 collective-permute-start.3
  15.9 1.0 collective-permute-done.3
  17.0 1.5 pad_maximum_fusion.2
  18.4 3.0 fusion.34
  28.1 9.8 %all-to-all-start = ((f32[8,2,8,2048]{3,2,1,0:T(8,128)}), f32[8,2,8,2048]{3,2,1,0:T(8,128)S(1)}, u32[]{:S(2)}, u32[]{:S(2)}) async-start(f32[8,2,8,2048]{3,2,1,0:T(8,128)} %fusion.98), calls=%async_computation | async-start | bytes 2097152 | tf_op jit(solution)/shard_map/all_to_all | solution.py:122
  39.0 28.0 %all-to-all-done = f32[8,2,8,2048]{3,2,1,0:T(8,128)S(1)} async-done(((f32[8,2,8,2048]{3,2,1,0:T(8,128)}), f32[8,2,8,2048]{3,2,1,0:T(8,128)S(1)}, u32[]{:S(2)}, u32[]{:S(2)}) %all-to-all-start) | async-done | bytes 1048608 | tf_op jit(solution)/shard_map/all_to_all | solution.py:122
  67.5 1.1 fusion.150
  69.0 1.1 fusion.148
  70.1 1.1 fusion.13
  71.2 1.1 fusion.12
  72.4 1.2 fusion.100
  73.6 1.2 fusion.99
  74.8 1.3 fusion.10
  76.1 0.9 fusion.142
  76.9 1.5 fusion.11
  80.2 0.9 convolution_subtract_fusion.7
  83.8 0.9 stack_reshape.13
  85.8 1.1 pad_maximum_fusion
  86.9 14.7 %copy.148 = f32[2,8,16384]{1,0,2:T(2,128)} copy(f32[2,8,16384]{2,1,0:T(8,128)S(1)} %pad_maximum_fusion) | data formatting | bytes 2097152 | tf_op jit(solution)/shard_map/stack | solution.py:138
  101.6 28.3 %reshape.247 = f32[8,1,32768]{2,1,0:T(1,128)S(1)} reshape(f32[16384,2,8]{2,1,0:T(2,128)} %bitcast.206) | data formatting | bytes 2097152
  129.9 31.4 %all_to_all.40 = f32[8,1,32768]{2,1,0:T(1,128)S(1)} all-to-all(f32[8,1,32768]{2,1,0:T(1,128)S(1)} %reshape.247), channel_id=1, replica_groups=mesh['rows'=32,'cols'=8] {'cols'}, dimensions={0} | all-to-all | bytes 2097152 | tf_op jit(solution)/shard_map/all_to_all | solution.py:137
  161.9 3.2 reduce
  165.1 32.1 %reshape.248 = f32[16384,2,8]{2,1,0:T(2,128)} reshape(f32[8,32768]{1,0:T(8,128)S(1)} %reduce) | data formatting | bytes 2097152
  197.1 13.2 %copy.196 = f32[2,8,8,2048]{3,2,1,0:T(8,128)S(1)} copy(f32[2,8,8,2048]{1,0,3,2:T(2,128)} %bitcast.207) | data formatting | bytes 2097152 | tf_op jit(solution)/shard_map/all_to_all | solution.py:137
  210.5 0.9 fusion.47
  211.4 0.9 convolution_subtract_fusion.1
  212.4 1.9 collective-permute-start.5
  214.3 2.4 collective-permute-start.4
  216.7 2.6 collective-permute-done.4
  219.4 1.3 collective-permute-start.6
  220.7 4.0 collective-permute-start.7
  224.7 1.0 collective-permute-done.7
  226.1 1.8 multiply_reduce_fusion.1
  227.9 79.0 %all-reduce = (f32[]{:T(128)}, f32[]{:T(128)}) all-reduce(f32[]{:T(128)} %get-tuple-element.4, f32[]{:T(128)} %get-tuple-element.3), channel_id=1, replica_groups=mesh['rows'=32,'cols'=8] {'rows','cols'}, use_global_device_ids=true, to_apply=%region_1.2 | all-reduce | flops 2 | bytes 16 | tf_op jit(solution)/shard_map/psum | solution.py:167
  309.8 31.8 %all_to_all.41 = f32[8,2,8,2048]{3,2,1,0:T(8,128)S(1)} all-to-all(f32[8,2,8,2048]{3,2,1,0:T(8,128)S(1)} %fusion.96), channel_id=1, replica_groups=mesh['rows'=32,'cols'=8] {'cols'}, dimensions={0} | all-to-all | bytes 2097152 | tf_op jit(solution)/shard_map/all_to_all | solution.py:122
  342.1 1.1 fusion.138
  343.6 1.1 fusion.136
  344.7 1.1 fusion.7
  345.9 1.1 fusion.6
  347.0 1.2 fusion.104
  348.2 1.2 fusion.103
  349.4 1.3 fusion.4
  351.5 1.3 fusion.5
  352.8 1.3 fusion.133
  354.1 0.9 convolution_add_fusion.1
  355.0 0.9 convolution_subtract_fusion.3
  358.4 1.0 copy.167
  359.4 1.9 stack_reshape.15
  362.5 1.1 pad_maximum_fusion.1
  363.6 14.7 %copy.168 = f32[2,8,16384]{1,0,2:T(2,128)} copy(f32[2,8,16384]{2,1,0:T(8,128)S(1)} %pad_maximum_fusion.1) | data formatting | bytes 2097152 | tf_op jit(solution)/shard_map/stack | solution.py:138
  378.3 28.3 %reshape.249 = f32[8,1,32768]{2,1,0:T(1,128)S(1)} reshape(f32[16384,2,8]{2,1,0:T(2,128)} %bitcast.208) | data formatting | bytes 2097152
  406.6 28.8 %all_to_all.42 = f32[8,1,32768]{2,1,0:T(1,128)} all-to-all(f32[8,1,32768]{2,1,0:T(1,128)S(1)} %reshape.249), channel_id=1, replica_groups=mesh['rows'=32,'cols'=8] {'cols'}, dimensions={0} | all-to-all | bytes 2097152 | tf_op jit(solution)/shard_map/all_to_all | solution.py:137
  435.4 4.4 reduce.1
  439.8 32.1 %reshape.250 = f32[16384,2,8]{2,1,0:T(2,128)} reshape(f32[8,32768]{1,0:T(8,128)S(1)} %reduce.1) | data formatting | bytes 2097152
  471.9 13.2 %copy.197 = f32[2,8,8,2048]{3,2,1,0:T(8,128)S(1)} copy(f32[2,8,8,2048]{1,0,3,2:T(2,128)} %bitcast.209) | data formatting | bytes 2097152 | tf_op jit(solution)/shard_map/all_to_all | solution.py:137
  485.2 0.9 fusion.44
  486.1 1.6 multiply_reduce_fusion
  487.7 76.6 %psum.23 = f32[]{:T(128)} all-reduce(f32[]{:T(128)} %get-tuple-element.30), channel_id=1, replica_groups=mesh['rows'=32,'cols'=8] {'rows','cols'}, use_global_device_ids=true, to_apply=%region_5.6 | all-reduce | flops 1 | bytes 8 | tf_op jit(solution)/shard_map/psum | solution.py:173
  565.5 1.1 multiply_add_fusion
  (73 shorter events, 23.1 us)
Async XLA Ops:
  1.5 8.2 %collective-permute-start = (f32[2,2048]{1,0:T(2,128)S(1)}, f32[2,2048]{1,0:T(2,128)S(1)}, u32[]{:S(2)}, u32[]{:S(2)}) collective-permute-start(f32[2,2048]{1,0:T(2,128)S(1)} %get-tuple-element.28), channel_id=1, source_target_pairs={{8,0},{16,8},{24,16},{32,24},{40,32},{48,40},{56,48},{64,56},{72,6... | collective-permute-start | bytes 49160 | tf_op jit(solution)/shard_map/ppermute | solution.py:24
  6.7 3.1 collective-permute-start.1
  10.6 5.3 collective-permute-start.2
  11.9 5.0 collective-permute-start.3
  28.1 38.9 %all-to-all-start = ((f32[8,2,8,2048]{3,2,1,0:T(8,128)}), f32[8,2,8,2048]{3,2,1,0:T(8,128)S(1)}, u32[]{:S(2)}, u32[]{:S(2)}) async-start(f32[8,2,8,2048]{3,2,1,0:T(8,128)} %fusion.98), calls=%async_computation | async-start | bytes 2097152 | tf_op jit(solution)/shard_map/all_to_all | solution.py:122
  197.1 28.9 %copy-start = (f32[64,2048]{1,0:T(8,128)S(1)}, f32[64,2048]{1,0:T(8,128)}, u32[]{:S(2)}) copy-start(f32[64,2048]{1,0:T(8,128)} %param.3) | copy-start | bytes 1572868
  197.1 28.9 %copy-start.2 = (s32[64,2048]{1,0:T(8,128)S(1)}, s32[64,2048]{1,0:T(8,128)}, u32[]{:S(2)}) copy-start(s32[64,2048]{1,0:T(8,128)} %param.5) | copy-start | bytes 1572868
  212.4 4.3 collective-permute-start.5
  214.3 5.1 collective-permute-start.4
  219.4 5.3 collective-permute-start.6
  220.7 5.0 collective-permute-start.7
  308.2 177.9 %copy-start.1 = (f32[64,2048]{1,0:T(8,128)}, f32[64,2048]{1,0:T(8,128)S(1)}, u32[]{:S(2)}) copy-start(f32[64,2048]{1,0:T(8,128)S(1)} %multiply_subtract_fusion.2) | copy-start | bytes 1572868
